TPU v7x, 32 devices: a whole 2x2x4 slice. The times are simulated.
32 devices in a mesh: grp: 4 (over z), dev: 8 (over y, x, core).
Axes of the slice: x: 2, y: 2, z: 4, core: 2. Of those that a mesh axis runs over, the one named last changes fastest.
Arguments:
- amplitudes: bfloat16 [1024, 589824], P('dev', 'grp'), may hold values from -6 to 6
- singles: float32 [32, 768], replicated, may hold values from -5 to 5
- pair_source: int32 [1024], replicated, may hold values from 0 to 1023, each once
- integrals: bfloat16 [589824, 512], P(('grp', 'dev')), may hold values from -0.0078125 to 0.0078125
Outputs:
- ladder: float32 [1024, 512], P('dev')
Inputs may be any that keep to these rules, and one draw needn't show every extreme that they name: `pair_source`: each occupied pair appears exactly once.
All inputs are finite; a program needn't handle non-finite values.
Results may differ from a plain program's by a relative error of at most 0.0029.
Values may be sent and summed in bfloat16 or wider, within the bound.
A program may use at most 320 MiB of HBM per device.

v0:
```python
import jax
import jax.numpy as jnp
from jax import lax
from jax.sharding import PartitionSpec as P


def body(amplitudes, singles, pair_source, integrals):
    local = lax.all_to_all(amplitudes, "dev", split_axis=1, concat_axis=0, tiled=True)
    occupied = singles.shape[0]
    virtual = singles.shape[1]
    count = local.shape[1]
    first = (lax.axis_index("grp") * lax.axis_size("dev") + lax.axis_index("dev")) * count
    cd_index = first + jnp.arange(count, dtype=jnp.int32)
    c_part = cd_index // virtual
    d_part = cd_index % virtual
    labels = jnp.arange(virtual, dtype=jnp.int32)[:, None]
    pick_c = (labels == c_part[None, :]).astype(jnp.float32)
    pick_d = (labels == d_part[None, :]).astype(jnp.float32)
    left_factor = jnp.dot(
        singles, pick_c, precision=lax.Precision.HIGHEST, preferred_element_type=jnp.float32
    )
    right_factor = jnp.dot(
        singles, pick_d, precision=lax.Precision.HIGHEST, preferred_element_type=jnp.float32
    )
    dressing = (left_factor[:, None, :] * right_factor[None, :, :]).reshape(
        occupied * occupied, count
    )
    ordered = jnp.take(local, pair_source, axis=0)
    tau = (ordered.astype(jnp.float32) + dressing).astype(jnp.bfloat16)
    share = occupied * occupied // lax.axis_size("dev")
    partial_value = jnp.dot(tau, integrals, preferred_element_type=jnp.float32)
    summed = lax.psum(partial_value, ("grp", "dev"))
    return lax.dynamic_slice_in_dim(summed, lax.axis_index("dev") * share, share, 0)


def solution(mesh):
    placed = (P("dev", "grp"), P(), P(), P(("grp", "dev"), None))
    return jax.shard_map(
        body, mesh=mesh, in_specs=placed, out_specs=P("dev", None), check_vma=False
    )
```

profile of v0, /device:TPU:0, one launch (start us, length us, event | category | flops | bytes accessed | tf_op | source)
XLA Modules:
  0.0 772.1 jit_solution(15173130806688675399)
XLA Ops:
  6.5 0.0 copy-start
  6.5 25.5 %copy.8 = bf16[16,8,8,18432]{3,2,0,1:T(8,128)(2,1)} copy(bf16[16,8,8,18432]{3,2,1,0:T(8,128)(2,1)} %bitcast.20) | data formatting | bytes 75497472 | tf_op jit(solution)/shard_map/all_to_all | solution.py:8
  32.0 0.0 copy-start.2
  32.0 7.7 all-to-all-start
  39.7 0.0 all-reduce.2.cloned.1.call-start
  39.8 0.0 copy-done.2
  39.8 0.1 add_select_fusion
  39.9 0.0 copy-done
  39.9 20.2 %fusion.5 = f32[32,18432]{1,0:T(8,128)S(1)} fusion(f32[32,768]{1,0:T(8,128)S(1)} %copy-done, s32[18432]{0:T(1024)S(1)} %get-tuple-element.5), kind=kOutput, calls=%fused_computation.11 | convolution fusion | flops 5449973760 | bytes 2531328 | tf_op jit(solution)/shard_map/dot_general | solution.py:22
  60.1 21.7 %fusion.6 = f32[32,18432]{1,0:T(8,128)} fusion(f32[32,768]{1,0:T(8,128)S(1)} %copy-done, s32[18432]{0:T(1024)S(1)} %get-tuple-element.6), kind=kOutput, calls=%fused_computation.12 | convolution fusion | flops 5449973760 | bytes 2531328 | tf_op jit(solution)/shard_map/dot_general | solution.py:19
  81.8 25.2 %broadcast_multiply_fusion = f32[32,32,18432]{2,1,0:T(8,128)} fusion(f32[32,18432]{1,0:T(8,128)S(1)} %fusion.5, f32[32,18432]{1,0:T(8,128)} %fusion.6), kind=kLoop, calls=%fused_computation.8 | loop fusion | flops 18874368 | bytes 80216064 | tf_op jit(solution)/shard_map/mul | solution.py:25
  107.0 341.9 %all-to-all-done = bf16[128,8,18432]{2,0,1:T(8,128)(2,1)} async-done(((bf16[128,8,18432]{2,0,1:T(8,128)(2,1)}), bf16[128,8,18432]{2,0,1:T(8,128)(2,1)}, u32[]{:S(2)}, u32[]{:S(2)}) %all-to-all-start) | async-done | bytes 37748768 | tf_op jit(solution)/shard_map/all_to_all | solution.py:8
  448.9 104.1 %gather_fusion = bf16[1024,18432]{1,0:T(8,128)(2,1)} fusion(bf16[1024,18432]{1,0:T(8,128)(2,1)} %bitcast.1, s32[1024]{0:T(1024)S(1)} %fusion.12), kind=kCustom, calls=%fused_computation | custom fusion | bytes 75501568 | tf_op jit(solution)/shard_map/jit(_take)/gather | solution.py:28
  553.0 0.0 copy-start.1
  553.0 47.7 %fusion = bf16[1024,18432]{1,0:T(8,128)(2,1)} fusion(f32[32,32,18432]{2,1,0:T(8,128)} %broadcast_multiply_fusion, bf16[1024,18432]{1,0:T(8,128)(2,1)} %gather_fusion, pred[1024]{0:T(1024)(128)(4,1)S(1)} %compare_and_fusion), kind=kLoop, calls=%fused_computation.2 | loop fusion | flops 75497472 | bytes 150995968 | tf_op jit(solution)/shard_map/convert_element_type | solution.py:29
  600.7 28.1 %fusion.13 = f32[1024,512]{1,0:T(8,128)} fusion(bf16[1024,18432]{1,0:T(8,128)(2,1)} %fusion, bf16[18432,512]{1,0:T(8,128)(2,1)} %param.7), kind=kOutput, calls=%fused_computation.26 | convolution fusion | flops 19327352832 | bytes 58720256 | tf_op jit(solution)/shard_map/dot_general | solution.py:31
  628.8 0.0 all-reduce.2.cloned.1.call-update
  628.8 134.3 %all-reduce.2.cloned.1.call-done = f32[1024,512]{1,0:T(8,128)} async-done(((f32[1024,512]{1,0:T(8,128)}), f32[1024,512]{1,0:T(8,128)}) %all-reduce.2.cloned.1.call-update) | async-done | bytes 2097168 | tf_op jit(solution)/shard_map/psum | solution.py:32
  763.1 1.7 constant_dynamic-slice_fusion
  764.8 0.0 copy-done.1
  (2 shorter events, 0.0 us)
Async XLA Ops:
  6.5 33.3 %copy-start = (f32[32,768]{1,0:T(8,128)S(1)}, f32[32,768]{1,0:T(8,128)}, u32[]{:S(2)}) copy-start(f32[32,768]{1,0:T(8,128)} %param.5) | copy-start | bytes 294916
  32.0 7.7 %copy-start.2 = (s32[1024]{0:T(1024)S(1)}, s32[1024]{0:T(1024)}, u32[]{:S(2)}) copy-start(s32[1024]{0:T(1024)} %param.6) | copy-start | bytes 12292
  32.0 416.9 %all-to-all-start = ((bf16[128,8,18432]{2,0,1:T(8,128)(2,1)}), bf16[128,8,18432]{2,0,1:T(8,128)(2,1)}, u32[]{:S(2)}, u32[]{:S(2)}) async-start(bf16[128,8,18432]{2,0,1:T(8,128)(2,1)} %bitcast.19), calls=%async_computation | async-start | bytes 75497472 | tf_op jit(solution)/shard_map/all_to_all | solution.py:8
  39.7 723.4 %all-reduce.2.cloned.1.call-start = ((), (), s32[]{:S(2)}) async-start(), calls=%async_computation.1 | async-start | bytes 4194304 | tf_op jit(solution)/shard_map/psum | solution.py:32
  553.0 211.8 %copy-start.1 = (f32[32,768]{1,0:T(8,128)S(1)}, f32[32,768]{1,0:T(8,128)}, u32[]{:S(2)}) copy-start(f32[32,768]{1,0:T(8,128)} %param.5) | copy-start | bytes 294916
Sparse Core Ops, SparseCore 0:
  629.0 134.1 all-reduce.1
where the time goes:
time: 781 us; the launch traced here: 772 us
  waiting for transfers between devices  476 us (61%)
  local copies, waits for them, and re-layouts  131 us (17%)
  other arithmetic  73 us (9%)
  matrix products  70 us (9%)
  between operations  13.9 us (2%)
    all_to_all x1, waiting for transfers between devices, body(): lax.all_to_all(amplitudes, 'dev', split_axis=1, concat_axis=0, tiled=True)  342 us
    psum x1, waiting for transfers between devices, body(): summed = lax.psum(partial_value, ('grp', 'dev'))  134 us
    gather x1, local copies, waits for them, and re-layouts, body(): ordered = jnp.take(local, pair_source, axis=0)  104 us
    convert_element_type x1, other arithmetic, body(): tau = (ordered.astype(jnp.float32) + dressing).astype(jnp.bfloat16)  47.7 us
    dot_general x1, matrix products, body(): partial_value = jnp.dot(tau, integrals, preferred_element_type=jnp.float32)  28.1 us
    all_to_all x1, local copies, waits for them, and re-layouts, body(): lax.all_to_all(amplitudes, 'dev', split_axis=1, concat_axis=0, tiled=True)  25.5 us
    mul x1, other arithmetic, body(): left_factor[:, None, :] * right_factor[None, :, :]  25.2 us
    dot_general x1, matrix products, body(): jnp.dot(singles, pick_c, precision=lax.Precision.HIGHEST, preferred_eleme...  21.7 us
  transfers between devices with their start and end apart: 2, of which 2 were waited for; matrix products, arithmetic and copies ran while one was open for 9% of the time, Pallas kernels for 0%

commit v1 on v0

v1 whole, which is shorter than its diff:
```python
import functools

import jax
import jax.numpy as jnp
from jax import lax
from jax.experimental import pallas as pl
from jax.experimental.pallas import tpu as pltpu
from jax.sharding import PartitionSpec as P

MESH = pl.DeviceIdType.MESH
CHUNK = 16
WINDOW = 2


def kernel(n, occupied, virtual, amp, integrals, pair, column, out, dress, recv,
           held, tile, total, send_sem, recv_sem, load_sem, held_sem):
    me = lax.axis_index("dev")
    rows = out.shape[1]
    count = integrals.shape[0]
    width = integrals.shape[1]
    chunks = rows // CHUNK
    blocks = count // virtual
    window = min(WINDOW, chunks)

    load_integrals = pltpu.make_async_copy(integrals, held, held_sem)
    load_integrals.start()

    barrier = pltpu.get_barrier_semaphore()
    for o in range(1, n):
        pl.semaphore_signal(barrier, inc=1, device_id={"dev": lax.rem(me + o, n)}, device_id_type=MESH)
    pl.semaphore_wait(barrier, n - 1)

    def span(q):
        return pl.ds(pl.multiple_of(q * CHUNK, CHUNK), CHUNK)

    def remote(o, q):
        peer = lax.rem(me + o, n)
        return pltpu.make_async_remote_copy(
            src_ref=amp.at[span(q), pl.ds(pl.multiple_of(peer * count, 128), count)],
            dst_ref=recv.at[o - 1, span(q), :],
            send_sem=send_sem.at[o - 1, q],
            recv_sem=recv_sem.at[o - 1, q],
            device_id={"dev": peer},
            device_id_type=MESH,
        )

    def load(o, q):
        if o == 0:
            source = amp.at[span(q), pl.ds(pl.multiple_of(me * count, 128), count)]
        else:
            source = recv.at[o - 1, span(q), :]
        return pltpu.make_async_copy(source, tile.at[lax.rem(me - o + n, n)], load_sem.at[o])

    order = list(range(n - 1, 0, -1))
    for q in range(window):
        for o in order:
            remote(o, q).start()

    dress[...] = jnp.zeros_like(dress)
    load_integrals.wait()

    def dress_one(c, carry):
        both = jnp.dot(pair[...], held[pl.ds(pl.multiple_of(c * virtual, virtual), virtual), :],
                       preferred_element_type=jnp.float32)
        inner = both[:occupied] + both[occupied:]

        def one_row(i, carry):
            dress[i] += column[c, i] * inner
            return carry

        return lax.fori_loop(0, occupied, one_row, carry)

    lax.fori_loop(0, blocks, dress_one, 0)

    def chunk(q, carry):
        for o in order:
            remote(o, q).wait_send()

        @pl.when(q + window < chunks)
        def _():
            for o in order:
                remote(o, q + window).start()

        for o in order:
            remote(o, q).wait_recv()
        for o in range(n):
            load(o, q).start()
        for o in range(n):
            load(o, q).wait()
        total[...] = jnp.zeros_like(total)

        def term(k, carry):
            part = pl.ds(pl.multiple_of(k * virtual, virtual), virtual)
            total[...] += jnp.dot(tile[:, :, part].reshape(n * CHUNK, virtual), held[part, :],
                                  preferred_element_type=jnp.float32)
            return carry

        lax.fori_loop(0, blocks, term, 0)
        out[:, span(q), :] = total[...].reshape(n, CHUNK, width)
        return carry

    lax.fori_loop(0, chunks, chunk, 0)


def split_pair(singles):
    high = lax.reduce_precision(singles, 8, 7)
    low = lax.reduce_precision(singles - high, 8, 7)
    return jnp.concatenate([high, low], 0).astype(jnp.bfloat16)


def body(amplitudes, singles, pair_source, integrals):
    n = lax.axis_size("dev")
    occupied, virtual = singles.shape
    rows = amplitudes.shape[0]
    count, width = integrals.shape
    chunks = rows // CHUNK
    blocks = count // virtual
    first = (lax.axis_index("grp") * n + lax.axis_index("dev")) * blocks
    column = lax.dynamic_slice_in_dim(singles.T, first, blocks, 0)
    any_spec = pl.BlockSpec(memory_space=pl.ANY)
    vmem = pl.BlockSpec(memory_space=pltpu.VMEM)
    smem = pl.BlockSpec(memory_space=pltpu.SMEM)
    partial, dress, _ = pl.pallas_call(
        functools.partial(kernel, n, occupied, virtual),
        out_shape=(
            jax.ShapeDtypeStruct((n, rows, width), jnp.float32),
            jax.ShapeDtypeStruct((occupied, occupied, width), jnp.float32),
            jax.ShapeDtypeStruct((n - 1, rows, count), jnp.bfloat16),
        ),
        in_specs=[any_spec, any_spec, vmem, smem],
        out_specs=(vmem, vmem, any_spec),
        scratch_shapes=[
            pltpu.VMEM((count, width), jnp.bfloat16),
            pltpu.VMEM((n, CHUNK, count), jnp.bfloat16),
            pltpu.VMEM((n * CHUNK, width), jnp.float32),
            pltpu.SemaphoreType.DMA((n - 1, chunks)),
            pltpu.SemaphoreType.DMA((n - 1, chunks)),
            pltpu.SemaphoreType.DMA((n,)),
            pltpu.SemaphoreType.DMA,
        ],
        compiler_params=pltpu.CompilerParams(
            collective_id=0, has_side_effects=True, vmem_limit_bytes=48 * 1024 * 1024
        ),
        cost_estimate=pl.CostEstimate(
            flops=2 * n * rows * count * width,
            bytes_accessed=4 * n * rows * count + 2 * count * width,
            transcendentals=0,
        ),
    )(amplitudes, integrals, split_pair(singles), column)
    whole = jnp.take(partial.reshape(n * rows, width), pair_source, axis=0)
    whole = whole + dress.reshape(n * rows, width)
    mine = lax.psum_scatter(whole, "dev", scatter_dimension=0, tiled=True)
    return lax.psum(mine, "grp")


def solution(mesh):
    placed = (P("dev", "grp"), P(), P(), P(("grp", "dev"), None))
    return jax.shard_map(
        body, mesh=mesh, in_specs=placed, out_specs=P("dev", None), check_vma=False
    )
```

time: 781 us -> 530 us (0.68); the launches traced: 772 us -> 529 us
  Pallas kernels: 0 us -> 421 us
  waiting for transfers between devices: 476 us -> 79.4 us
  local copies, waits for them, and re-layouts: 131 us -> 8.81 us
  matrix products: 70 us -> 0 us
  other arithmetic: 73 us -> 6.1 us
    pallas_call x0 -> x1, Pallas kernels: none -> 421 us  [body(): pl.pallas_call(functools.partial(kernel, n, occupied, virtual), out_shape...]
    all_to_all x1 -> x0, waiting for transfers between devices: 342 us -> none  [body(): lax.all_to_all(amplitudes, 'dev', split_axis=1, concat_axis=0, tiled=True)]
    gather x1, local copies, waits for them, and re-layouts: 104 us -> 4.91 us  [body(): whole = jnp.take(partial.reshape(n * rows, width), pair_source, axis=0)]
    psum x1, waiting for transfers between devices: 134 us -> 37.8 us  [body(): return lax.psum(mine, 'grp')]
    dot_general x3 -> x0, matrix products: 70 us -> none  [the longest x1 28.1 us: body(): partial_value = jnp.dot(tau, integrals, preferred_element_type=jnp.float32)]
    convert_element_type x1 -> x0, other arithmetic: 47.7 us -> none  [body(): tau = (ordered.astype(jnp.float32) + dressing).astype(jnp.bfloat16)]
    reduce_scatter x0 -> x1, waiting for transfers between devices: none -> 41.6 us  [body(): mine = lax.psum_scatter(whole, 'dev', scatter_dimension=0, tiled=True)]
    all_to_all x1 -> x0, local copies, waits for them, and re-layouts: 25.5 us -> none  [body(): lax.all_to_all(amplitudes, 'dev', split_axis=1, concat_axis=0, tiled=True)]
  transfers between devices with their start and end apart: 2 -> 2, of which waited for: 2 -> 2; matrix products, arithmetic and copies ran while one was open for 9% -> 0% of each run, Pallas kernels for 0% -> 0%
where the time goes in v1:
time: 530 us; the launch traced here: 529 us
  Pallas kernels  421 us (79%)
  waiting for transfers between devices  79.4 us (15%)
  between operations  13.4 us (3%)
  local copies, waits for them, and re-layouts  8.81 us (2%)
  other arithmetic  6.1 us (1%)
    pallas_call x1, Pallas kernels, body(): pl.pallas_call(functools.partial(kernel, n, occupied, virtual), out_shape...  421 us
    reduce_scatter x1, waiting for transfers between devices, body(): mine = lax.psum_scatter(whole, 'dev', scatter_dimension=0, tiled=True)  41.6 us
    psum x1, waiting for transfers between devices, body(): return lax.psum(mine, 'grp')  37.8 us
  transfers between devices with their start and end apart: 2, of which 2 were waited for; matrix products, arithmetic and copies ran while one was open for 0% of the time, Pallas kernels for 0%

profile of v1, /device:TPU:0, one launch (start us, length us, event | category | flops | bytes accessed | tf_op | source)
XLA Modules:
  0.0 529.2 jit_solution(14710264470988411326)
XLA Ops:
  6.5 0.0 reduce-scatter.2.cloned.1.call-start
  6.5 0.7 fusion.2
  7.2 0.7 compare_and_fusion
  7.9 0.9 reduce-precision_convert_fusion
  8.8 0.8 constant_dynamic-slice_fusion
  9.7 0.1 copy.6
  9.8 421.3 %shard_map.46 = (f32[8,128,512]{2,1,0:T(8,128)S(1)}, f32[32,32,512]{2,1,0:T(8,128)S(1)}, bf16[7,128,18432]{2,1,0:T(8,128)(2,1)}) custom-call(bf16[128,147456]{1,0:T(8,128)(2,1)} %amp.1, bf16[18432,512]{1,0:T(8,128)(2,1)} %integrals.1, bf16[64,768]{1,0:T(8,128)(2,1)S(1)} %pad_maximum_fusion.pair, f32[24,32]{1,0:T(8,128)S(1)} %bitcast.5), custom_call_target="tpu_custom_call" | custom-call | flops 19327352832 | bytes 94371840 | tf_op jit(solution)/shard_map/pallas_call | solution.py:123
  431.1 0.0 copy-start
  431.1 1.3 copy-done
  432.5 4.9 gather_fusion
  437.4 3.8 bitcast_add_fusion
  441.2 0.0 reduce-scatter.2.cloned.1.call-update
  441.2 0.0 all-reduce.2.cloned.1.call-start
  441.2 41.6 %reduce-scatter.2.cloned.1.call-done = f32[128,512]{1,0:T(8,128)} async-done(((f32[1024,512]{1,0:T(8,128)}), f32[128,512]{1,0:T(8,128)}) %reduce-scatter.2.cloned.1.call-update) | async-done | bytes 262160 | tf_op jit(solution)/shard_map/reduce_scatter | solution.py:152
  482.9 0.0 all-reduce.2.cloned.1.call-update
  482.9 37.8 %all-reduce.2.cloned.1.call-done = f32[128,512]{1,0:T(8,128)} async-done(((f32[128,512]{1,0:T(8,128)}), f32[128,512]{1,0:T(8,128)}) %all-reduce.2.cloned.1.call-update) | async-done | bytes 262160 | tf_op jit(solution)/shard_map/psum | solution.py:153
  520.7 1.7 copy.8
  (1 shorter events, 0.0 us)
Async XLA Ops:
  6.5 476.3 %reduce-scatter.2.cloned.1.call-start = ((), (), s32[]{:S(2)}) async-start(), calls=%async_computation.1 | async-start | bytes 2359296 | tf_op jit(solution)/shard_map/reduce_scatter | solution.py:152
  431.1 1.3 copy-start
  441.2 79.5 %all-reduce.2.cloned.1.call-start = ((), (), s32[]{:S(2)}) async-start(), calls=%async_computation.2 | async-start | bytes 524288 | tf_op jit(solution)/shard_map/psum | solution.py:153
Sparse Core Ops, SparseCore 0:
  441.3 41.5 reduce-scatter.1
  485.3 35.2 all-reduce.1

commit v2 on v1

--- a/solution.py
+++ b/solution.py
@@ -149,8 +149,9 @@
     )(amplitudes, integrals, split_pair(singles), column)
     whole = jnp.take(partial.reshape(n * rows, width), pair_source, axis=0)
     whole = whole + dress.reshape(n * rows, width)
-    mine = lax.psum_scatter(whole, "dev", scatter_dimension=0, tiled=True)
-    return lax.psum(mine, "grp")
+    whole = whole.reshape(n, n * rows // n, width)
+    mine = lax.all_to_all(whole, "dev", split_axis=0, concat_axis=0, tiled=True).sum(0)
+    return lax.all_gather(mine, "grp").sum(0)
 
 
 def solution(mesh):

time: 530 us -> 507 us (0.957)
  waiting for transfers between devices: 79.4 us -> 27.4 us
  blocking collectives: 0 us -> 29.2 us
    reduce_scatter x1 -> x0, waiting for transfers between devices: 41.6 us -> none  [body(): mine = lax.psum_scatter(whole, 'dev', scatter_dimension=0, tiled=True)]
    psum x1 -> x0, waiting for transfers between devices: 37.8 us -> none  [body(): return lax.psum(mine, 'grp')]
    all_to_all x0 -> x1, blocking collectives: none -> 29.2 us  [body(): lax.all_to_all(whole, 'dev', split_axis=0, concat_axis=0, tiled=True).sum(0)]
    all_gather x0 -> x1, waiting for transfers between devices: none -> 27.4 us  [body(): return lax.all_gather(mine, 'grp').sum(0)]
  transfers between devices with their start and end apart: 2 -> 1, of which waited for: 2 -> 1; matrix products, arithmetic and copies ran while one was open for 0% -> 0% of each run, Pallas kernels for 0% -> 0%
where the time goes in v2:
time: 507 us; the launch traced here: 506 us
  Pallas kernels  421 us (83%)
  blocking collectives  29.2 us (6%)
  waiting for transfers between devices  27.4 us (5%)
  between operations  13.4 us (3%)
  other arithmetic  7.73 us (2%)
  local copies, waits for them, and re-layouts  7.1 us (1%)
    pallas_call x1, Pallas kernels, body(): pl.pallas_call(functools.partial(kernel, n, occupied, virtual), out_shape...  421 us
    all_to_all x1, blocking collectives, body(): lax.all_to_all(whole, 'dev', split_axis=0, concat_axis=0, tiled=True).sum(0)  29.2 us
    all_gather x1, waiting for transfers between devices, body(): return lax.all_gather(mine, 'grp').sum(0)  27.4 us
  transfers between devices with their start and end apart: 1, of which 1 were waited for; matrix products, arithmetic and copies ran while one was open for 0% of the time, Pallas kernels for 0%

profile of v2, /device:TPU:0, one launch (start us, length us, event | category | flops | bytes accessed | tf_op | source)
XLA Modules:
  0.0 506.3 jit_solution(13290220281446746394)
XLA Ops:
  6.5 0.0 all-gather.3.cloned.1.call-start
  6.5 0.7 fusion.2
  7.2 0.7 and_bitcast_fusion
  7.9 0.9 reduce-precision_convert_fusion
  8.8 0.8 constant_dynamic-slice_fusion
  9.7 0.1 copy.7
  9.8 421.3 %shard_map.46 = (f32[8,128,512]{2,1,0:T(8,128)S(1)}, f32[32,32,512]{2,1,0:T(8,128)S(1)}, bf16[7,128,18432]{2,1,0:T(8,128)(2,1)}) custom-call(bf16[128,147456]{1,0:T(8,128)(2,1)} %amp.1, bf16[18432,512]{1,0:T(8,128)(2,1)} %integrals.1, bf16[64,768]{1,0:T(8,128)(2,1)S(1)} %pad_maximum_fusion.pair, f32[24,32]{1,0:T(8,128)S(1)} %bitcast.11), custom_call_target="tpu_custom_call" | custom-call | flops 19327352832 | bytes 94371840 | tf_op jit(solution)/shard_map/pallas_call | solution.py:123
  431.1 0.0 copy-start
  431.1 1.3 copy-done
  432.4 4.9 gather_fusion
  437.3 2.5 bitcast_add_fusion
  439.8 29.2 %all_to_all.5 = f32[8,128,512]{2,1,0:T(8,128)S(1)} all-to-all(f32[8,128,512]{2,1,0:T(8,128)S(1)} %bitcast_add_fusion), channel_id=1, replica_groups=mesh['grp'=4,'dev'=8] {'dev'}, dimensions={0} | all-to-all | bytes 4194304 | tf_op jit(solution)/shard_map/all_to_all | solution.py:153
  469.0 0.9 reduce_sum.18
  470.0 0.0 all-gather.3.cloned.1.call-update
  470.0 27.4 %all-gather.3.cloned.1.call-done = f32[512,512]{1,0:T(8,128)} async-done(((f32[128,512]{1,0:T(8,128)}), f32[512,512]{1,0:T(8,128)}) %all-gather.3.cloned.1.call-update) | async-done | bytes 1048592 | tf_op jit(solution)/shard_map/all_gather | solution.py:154
  497.4 2.0 reduce_sum.19
  (1 shorter events, 0.0 us)
Async XLA Ops:
  6.5 490.9 %all-gather.3.cloned.1.call-start = ((), (), s32[]{:S(2)}) async-start(), calls=%async_computation.1 | async-start | bytes 1310720 | tf_op jit(solution)/shard_map/all_gather | solution.py:154
  431.1 1.3 copy-start
Sparse Core Ops, SparseCore 0:
  470.1 27.2 all-gather.2

commit v3 on v1

--- a/solution.py
+++ b/solution.py
@@ -100,6 +100,122 @@
         return carry
 
     lax.fori_loop(0, chunks, chunk, 0)
+
+
+def combine(n, g, whole, out, half, summed, got, mine, zgot, full,
+            half_send, half_recv, got_send, got_recv, z_send, z_recv, full_send, full_recv):
+    me = lax.axis_index("dev")
+    z = lax.axis_index("grp")
+    m = n // 2
+    side = lax.rem(me, 2)
+    base = me // 2
+    mate = me + 1 - 2 * side
+    piece = out.shape[0] // g
+
+    def peer(o):
+        return 2 * lax.rem(base + o, m) + side
+
+    def zpeer(o):
+        return lax.rem(z + o, g)
+
+    barrier = pltpu.get_barrier_semaphore()
+    for target in [mate] + [peer(o) for o in range(1, m)]:
+        pl.semaphore_signal(barrier, inc=1, device_id={"dev": target}, device_id_type=MESH)
+    for o in range(1, g):
+        pl.semaphore_signal(barrier, inc=1, device_id={"grp": zpeer(o)}, device_id_type=MESH)
+    pl.semaphore_wait(barrier, 1 + (m - 1) + (g - 1))
+
+    def slab(i):
+        return pl.ds(pl.multiple_of(i * piece, piece), piece)
+
+    def to_mate(o):
+        return pltpu.make_async_remote_copy(
+            src_ref=whole.at[lax.rem(base + o, m), 1 - side], dst_ref=half.at[o],
+            send_sem=half_send.at[o], recv_sem=half_recv.at[o],
+            device_id={"dev": mate}, device_id_type=MESH)
+
+    def to_peer(o):
+        return pltpu.make_async_remote_copy(
+            src_ref=summed.at[o], dst_ref=got.at[o - 1],
+            send_sem=got_send.at[o - 1], recv_sem=got_recv.at[o - 1],
+            device_id={"dev": peer(o)}, device_id_type=MESH)
+
+    def to_owner(o):
+        return pltpu.make_async_remote_copy(
+            src_ref=mine.at[slab(zpeer(o)), :], dst_ref=zgot.at[o - 1],
+            send_sem=z_send.at[o - 1], recv_sem=z_recv.at[o - 1],
+            device_id={"grp": zpeer(o)}, device_id_type=MESH)
+
+    def to_all(o, slot):
+        return pltpu.make_async_remote_copy(
+            src_ref=full.at[slab(slot), :], dst_ref=full.at[slab(slot), :],
+            send_sem=full_send.at[o - 1], recv_sem=full_recv.at[o - 1],
+            device_id={"grp": zpeer(o)}, device_id_type=MESH)
+
+    order = list(range(1, m)) + [0]
+    for o in order:
+        to_mate(o).start()
+    for o in order:
+        to_mate(o).wait_recv()
+        summed[o] = whole[lax.rem(base + o, m), side] + half[o]
+        if o:
+            to_peer(o).start()
+    value = summed[0]
+    for o in range(1, m):
+        to_peer(o).wait_recv()
+        value = value + got[o - 1]
+    mine[...] = value
+    for o in range(1, g):
+        to_owner(o).start()
+    part = mine[slab(z), :]
+    for o in range(1, g):
+        to_owner(o).wait_recv()
+        part = part + zgot[o - 1]
+    full[slab(z), :] = part
+    for o in range(1, g):
+        to_all(o, z).start()
+    for o in range(1, g):
+        to_all(o, lax.rem(z - o + g, g)).wait_recv()
+    for o in order:
+        to_mate(o).wait_send()
+    for o in range(1, m):
+        to_peer(o).wait_send()
+    for o in range(1, g):
+        to_owner(o).wait_send()
+        to_all(o, z).wait_send()
+    out[...] = full[...]
+
+
+def reduce_devices(whole):
+    n, g = lax.axis_size("dev"), lax.axis_size("grp")
+    share, width = whole.shape[0] // n, whole.shape[1]
+    if n % 2 or n < 4 or g < 2 or share % (8 * g):
+        whole = whole.reshape(n, share, width)
+        mine = lax.all_to_all(whole, "dev", split_axis=0, concat_axis=0, tiled=True).sum(0)
+        return lax.all_gather(mine, "grp").sum(0)
+    m = n // 2
+    vmem = pl.BlockSpec(memory_space=pltpu.VMEM)
+    f32 = jnp.float32
+    dma = pltpu.SemaphoreType.DMA
+    return pl.pallas_call(
+        functools.partial(combine, n, g),
+        out_shape=jax.ShapeDtypeStruct((share, width), f32),
+        in_specs=[vmem],
+        out_specs=vmem,
+        scratch_shapes=[
+            pltpu.VMEM((m, share, width), f32),
+            pltpu.VMEM((m, share, width), f32),
+            pltpu.VMEM((m - 1, share, width), f32),
+            pltpu.VMEM((share, width), f32),
+            pltpu.VMEM((g - 1, share // g, width), f32),
+            pltpu.VMEM((share, width), f32),
+            dma((m,)), dma((m,)), dma((m - 1,)), dma((m - 1,)),
+            dma((g - 1,)), dma((g - 1,)), dma((g - 1,)), dma((g - 1,)),
+        ],
+        compiler_params=pltpu.CompilerParams(
+            collective_id=1, has_side_effects=True, vmem_limit_bytes=32 * 1024 * 1024
+        ),
+    )(whole.reshape(m, 2, share, width))
 
 
 def split_pair(singles):
@@ -149,8 +265,7 @@
     )(amplitudes, integrals, split_pair(singles), column)
     whole = jnp.take(partial.reshape(n * rows, width), pair_source, axis=0)
     whole = whole + dress.reshape(n * rows, width)
-    mine = lax.psum_scatter(whole, "dev", scatter_dimension=0, tiled=True)
-    return lax.psum(mine, "grp")
+    return reduce_devices(whole)
 
 
 def solution(mesh):

time: 530 us -> 463 us (0.87)
  waiting for transfers between devices: 79.4 us -> 0 us
  Pallas kernels: 421 us -> 452 us
  between operations: 13.4 us -> 0.06 us
    reduce_scatter x1 -> x0, waiting for transfers between devices: 41.6 us -> none  [body(): mine = lax.psum_scatter(whole, 'dev', scatter_dimension=0, tiled=True)]
    psum x1 -> x0, waiting for transfers between devices: 37.8 us -> none  [body(): return lax.psum(mine, 'grp')]
    pallas_call x0 -> x1, Pallas kernels: none -> 30.5 us  [reduce_devices(): pl.pallas_call(functools.partial(combine, n, g), out_shape=jax.ShapeDtype...]
  transfers between devices with their start and end apart: 2 -> 0, of which waited for: 2 -> 0; matrix products, arithmetic and copies ran while one was open for 0% -> 0% of each run, Pallas kernels for 0% -> 0%
where the time goes in v3:
time: 463 us
  Pallas kernels  452 us (98%)
  local copies, waits for them, and re-layouts  7.86 us (2%)
    pallas_call x1, Pallas kernels, body(): pl.pallas_call(functools.partial(kernel, n, occupied, virtual), out_shape...  421 us
    pallas_call x1, Pallas kernels, reduce_devices(): pl.pallas_call(functools.partial(combine, n, g), out_shape=jax.ShapeDtype...  30.5 us

profile of v3, /device:TPU:0, one launch (start us, length us, event | category | flops | bytes accessed | tf_op | source)
XLA Modules:
  0.0 463.2 jit_solution(10823781923205909499)
XLA Ops:
  0.0 0.8 constant_dynamic-slice_fusion
  0.8 0.1 copy.7
  0.9 0.9 reduce-precision_convert_fusion
  1.8 0.0 copy-start.1
  1.8 421.4 %shard_map.46 = (f32[8,128,512]{2,1,0:T(8,128)S(1)}, f32[32,32,512]{2,1,0:T(8,128)S(1)}, bf16[7,128,18432]{2,1,0:T(8,128)(2,1)}) custom-call(bf16[128,147456]{1,0:T(8,128)(2,1)} %amp.1, bf16[18432,512]{1,0:T(8,128)(2,1)} %integrals.1, bf16[64,768]{1,0:T(8,128)(2,1)S(1)} %pad_maximum_fusion.pair, f32[24,32]{1,0:T(8,128)S(1)} %bitcast.6), custom_call_target="tpu_custom_call" | custom-call | flops 19327352832 | bytes 94371840 | tf_op jit(solution)/shard_map/pallas_call | solution.py:239
  423.2 0.0 copy-start
  423.2 1.3 copy-done
  424.5 0.0 copy-done.1
  424.6 4.9 %gather_fusion = f32[1024,512]{1,0:T(8,128)} fusion(f32[1024,512]{1,0:T(8,128)S(1)} %bitcast.4, s32[1024]{0:T(1024)S(1)} %fusion.2), kind=kCustom, calls=%fused_computation | custom fusion | bytes 4198400 | tf_op jit(solution)/shard_map/jit(_take)/gather | solution.py:266
  429.5 2.5 select_add_fusion.whole
  432.0 30.5 %shard_map.47 = f32[128,512]{1,0:T(8,128)S(1)} custom-call(f32[4,2,128,512]{3,2,1,0:T(8,128)S(1)} %select_add_fusion.whole), custom_call_target="tpu_custom_call" | custom-call | tf_op jit(solution)/shard_map/pallas_call | solution.py:200
  462.5 0.7 copy.9
  (4 shorter events, 0.0 us)
Async XLA Ops:
  1.8 422.7 %copy-start.1 = (s32[1024]{0:T(1024)S(1)}, s32[1024]{0:T(1024)}, u32[]{:S(2)}) copy-start(s32[1024]{0:T(1024)} %param.6) | copy-start | bytes 12292
  423.2 1.3 copy-start

commit v4 on v3

--- a/solution.py
+++ b/solution.py
@@ -10,6 +10,7 @@
 MESH = pl.DeviceIdType.MESH
 CHUNK = 16
 WINDOW = 2
+PARTS = 2
 
 
 def kernel(n, occupied, virtual, amp, integrals, pair, column, out, dress, recv,
@@ -111,6 +112,10 @@
     base = me // 2
     mate = me + 1 - 2 * side
     piece = out.shape[0] // g
+    wide = out.shape[1] // PARTS
+
+    def cols(h):
+        return pl.ds(h * wide, wide)
 
     def peer(o):
         return 2 * lax.rem(base + o, m) + side
@@ -128,68 +133,73 @@
     def slab(i):
         return pl.ds(pl.multiple_of(i * piece, piece), piece)
 
-    def to_mate(o):
-        return pltpu.make_async_remote_copy(
-            src_ref=whole.at[lax.rem(base + o, m), 1 - side], dst_ref=half.at[o],
-            send_sem=half_send.at[o], recv_sem=half_recv.at[o],
+    def to_mate(o, h):
+        return pltpu.make_async_remote_copy(
+            src_ref=whole.at[lax.rem(base + o, m), 1 - side, :, cols(h)], dst_ref=half.at[o, :, cols(h)],
+            send_sem=half_send.at[o, h], recv_sem=half_recv.at[o, h],
             device_id={"dev": mate}, device_id_type=MESH)
 
-    def to_peer(o):
-        return pltpu.make_async_remote_copy(
-            src_ref=summed.at[o], dst_ref=got.at[o - 1],
-            send_sem=got_send.at[o - 1], recv_sem=got_recv.at[o - 1],
+    def to_peer(o, h):
+        return pltpu.make_async_remote_copy(
+            src_ref=summed.at[o, :, cols(h)], dst_ref=got.at[o - 1, :, cols(h)],
+            send_sem=got_send.at[o - 1, h], recv_sem=got_recv.at[o - 1, h],
             device_id={"dev": peer(o)}, device_id_type=MESH)
 
-    def to_owner(o):
-        return pltpu.make_async_remote_copy(
-            src_ref=mine.at[slab(zpeer(o)), :], dst_ref=zgot.at[o - 1],
-            send_sem=z_send.at[o - 1], recv_sem=z_recv.at[o - 1],
+    def to_owner(o, h):
+        return pltpu.make_async_remote_copy(
+            src_ref=mine.at[slab(zpeer(o)), cols(h)], dst_ref=zgot.at[o - 1, :, cols(h)],
+            send_sem=z_send.at[o - 1, h], recv_sem=z_recv.at[o - 1, h],
             device_id={"grp": zpeer(o)}, device_id_type=MESH)
 
-    def to_all(o, slot):
-        return pltpu.make_async_remote_copy(
-            src_ref=full.at[slab(slot), :], dst_ref=full.at[slab(slot), :],
-            send_sem=full_send.at[o - 1], recv_sem=full_recv.at[o - 1],
+    def to_all(o, slot, h):
+        return pltpu.make_async_remote_copy(
+            src_ref=full.at[slab(slot), cols(h)], dst_ref=full.at[slab(slot), cols(h)],
+            send_sem=full_send.at[o - 1, h], recv_sem=full_recv.at[o - 1, h],
             device_id={"grp": zpeer(o)}, device_id_type=MESH)
 
     order = list(range(1, m)) + [0]
-    for o in order:
-        to_mate(o).start()
-    for o in order:
-        to_mate(o).wait_recv()
-        summed[o] = whole[lax.rem(base + o, m), side] + half[o]
-        if o:
-            to_peer(o).start()
-    value = summed[0]
-    for o in range(1, m):
-        to_peer(o).wait_recv()
-        value = value + got[o - 1]
-    mine[...] = value
-    for o in range(1, g):
-        to_owner(o).start()
-    part = mine[slab(z), :]
-    for o in range(1, g):
-        to_owner(o).wait_recv()
-        part = part + zgot[o - 1]
-    full[slab(z), :] = part
-    for o in range(1, g):
-        to_all(o, z).start()
-    for o in range(1, g):
-        to_all(o, lax.rem(z - o + g, g)).wait_recv()
-    for o in order:
-        to_mate(o).wait_send()
-    for o in range(1, m):
-        to_peer(o).wait_send()
-    for o in range(1, g):
-        to_owner(o).wait_send()
-        to_all(o, z).wait_send()
+    for h in range(PARTS):
+        for o in order:
+            to_mate(o, h).start()
+    for h in range(PARTS):
+        for o in order:
+            to_mate(o, h).wait_recv()
+            summed[o, :, cols(h)] = whole[lax.rem(base + o, m), side, :, cols(h)] + half[o, :, cols(h)]
+            if o:
+                to_peer(o, h).start()
+    for h in range(PARTS):
+        value = summed[0, :, cols(h)]
+        for o in range(1, m):
+            to_peer(o, h).wait_recv()
+            value = value + got[o - 1, :, cols(h)]
+        mine[:, cols(h)] = value
+        for o in range(1, g):
+            to_owner(o, h).start()
+    for h in range(PARTS):
+        part = mine[slab(z), cols(h)]
+        for o in range(1, g):
+            to_owner(o, h).wait_recv()
+            part = part + zgot[o - 1, :, cols(h)]
+        full[slab(z), cols(h)] = part
+        for o in range(1, g):
+            to_all(o, z, h).start()
+    for h in range(PARTS):
+        for o in range(1, g):
+            to_all(o, lax.rem(z - o + g, g), h).wait_recv()
+        for o in order:
+            to_mate(o, h).wait_send()
+        for o in range(1, m):
+            to_peer(o, h).wait_send()
+        for o in range(1, g):
+            to_owner(o, h).wait_send()
+            to_all(o, z, h).wait_send()
     out[...] = full[...]
 
 
 def reduce_devices(whole):
     n, g = lax.axis_size("dev"), lax.axis_size("grp")
     share, width = whole.shape[0] // n, whole.shape[1]
-    if n % 2 or n < 4 or g < 2 or share % (8 * g):
+    if n % 2 or n < 4 or g < 2 or share % (8 * g) or width % (128 * PARTS):
         whole = whole.reshape(n, share, width)
         mine = lax.all_to_all(whole, "dev", split_axis=0, concat_axis=0, tiled=True).sum(0)
         return lax.all_gather(mine, "grp").sum(0)
@@ -209,8 +219,8 @@
             pltpu.VMEM((share, width), f32),
             pltpu.VMEM((g - 1, share // g, width), f32),
             pltpu.VMEM((share, width), f32),
-            dma((m,)), dma((m,)), dma((m - 1,)), dma((m - 1,)),
-            dma((g - 1,)), dma((g - 1,)), dma((g - 1,)), dma((g - 1,)),
+            dma((m, PARTS)), dma((m, PARTS)), dma((m - 1, PARTS)), dma((m - 1, PARTS)),
+            dma((g - 1, PARTS)), dma((g - 1, PARTS)), dma((g - 1, PARTS)), dma((g - 1, PARTS)),
         ],
         compiler_params=pltpu.CompilerParams(
             collective_id=1, has_side_effects=True, vmem_limit_bytes=32 * 1024 * 1024

time: 463 us -> 461 us (level)
  no operation moved by 1% of the time
where the time goes in v4:
time: 461 us; the launch traced here: 460 us
  Pallas kernels  449 us (97%)
  local copies, waits for them, and re-layouts  7.86 us (2%)
    pallas_call x1, Pallas kernels, body(): pl.pallas_call(functools.partial(kernel, n, occupied, virtual), out_shape...  421 us
    pallas_call x1, Pallas kernels, reduce_devices(): pl.pallas_call(functools.partial(combine, n, g), out_shape=jax.ShapeDtype...  27.7 us

profile of v4, /device:TPU:0, one launch (start us, length us, event | category | flops | bytes accessed | tf_op | source)
XLA Modules:
  0.0 460.4 jit_solution(8139490603151724332)
XLA Ops:
  0.0 0.8 constant_dynamic-slice_fusion
  0.8 0.1 copy.7
  0.9 0.9 reduce-precision_convert_fusion
  1.8 0.0 copy-start.1
  1.8 421.4 %shard_map.46 = (f32[8,128,512]{2,1,0:T(8,128)S(1)}, f32[32,32,512]{2,1,0:T(8,128)S(1)}, bf16[7,128,18432]{2,1,0:T(8,128)(2,1)}) custom-call(bf16[128,147456]{1,0:T(8,128)(2,1)} %amp.1, bf16[18432,512]{1,0:T(8,128)(2,1)} %integrals.1, bf16[64,768]{1,0:T(8,128)(2,1)S(1)} %pad_maximum_fusion.pair, f32[24,32]{1,0:T(8,128)S(1)} %bitcast.6), custom_call_target="tpu_custom_call" | custom-call | flops 19327352832 | bytes 94371840 | tf_op jit(solution)/shard_map/pallas_call | solution.py:249
  423.2 0.0 copy-start
  423.2 1.3 copy-done
  424.5 0.0 copy-done.1
  424.6 4.9 %gather_fusion = f32[1024,512]{1,0:T(8,128)} fusion(f32[1024,512]{1,0:T(8,128)S(1)} %bitcast.4, s32[1024]{0:T(1024)S(1)} %fusion.2), kind=kCustom, calls=%fused_computation | custom fusion | bytes 4198400 | tf_op jit(solution)/shard_map/jit(_take)/gather | solution.py:276
  429.5 2.5 select_add_fusion.whole
  432.0 27.7 %shard_map.47 = f32[128,512]{1,0:T(8,128)S(1)} custom-call(f32[4,2,128,512]{3,2,1,0:T(8,128)S(1)} %select_add_fusion.whole), custom_call_target="tpu_custom_call" | custom-call | tf_op jit(solution)/shard_map/pallas_call | solution.py:210
  459.7 0.7 copy.9
  (4 shorter events, 0.0 us)
Async XLA Ops:
  1.8 422.7 %copy-start.1 = (s32[1024]{0:T(1024)S(1)}, s32[1024]{0:T(1024)}, u32[]{:S(2)}) copy-start(s32[1024]{0:T(1024)} %param.6) | copy-start | bytes 12292
  423.2 1.3 copy-start
